TPU v7x, 256 devices: a whole 4x4x8 slice. The times are simulated.
256 devices in a mesh: stream: 32 (over x, z), span: 8 (over y, core).
Axes of the slice: x: 4, y: 4, z: 8, core: 2. Of those that a mesh axis runs over, the one named last changes fastest.
Arguments:
- state: float32 [5, 8, 512, 1024], P(None, None, 'stream', 'span'), may hold values from -0.3 to 3, as said below
Outputs:
- state_next: float32 [5, 8, 512, 1024], P(None, None, 'stream', 'span')
- flux_difference: float32 [5, 8, 512, 1024], P(None, None, 'stream', 'span')
Inputs may be any that keep to these rules, and one draw needn't show every extreme that they name: Each cell holds a gas state with density from 0.55 to 1.65, streamwise velocity from 0.2 to 0.6, spanwise and wall-normal velocities within 0.15 of zero and pressure from 0.55 to 1.0.
All inputs are finite; a program needn't handle non-finite values.
Results may differ from a plain program's by a relative error of at most 0.002.
Values sent between devices are 32-bit elements; how exact they have to be, the bound alone decides.
A program may use at most 128 MiB of HBM per device.

v0:
```python
import jax
import jax.numpy as jnp
from jax import lax
from jax.experimental import pallas as pl
from jax.experimental.pallas import tpu as pltpu
from jax.sharding import PartitionSpec as P

MESH = pl.DeviceIdType.MESH
N = 32
SPAN = 8
CX = 16
DISS = 1.0 / 256.0
DIAG = 1.25 / 819.2
PIVOTS = (1, 2, 3, 0, 4)
ROWS = 16
BACK_ROWS = 8
F32 = jnp.float32


def mul(a, b):
    if a is None or b is None:
        return None
    if isinstance(a, float) and a == 1.0:
        return b
    if isinstance(b, float) and b == 1.0:
        return a
    return a * b


def add(a, b):
    if a is None:
        return b
    if b is None:
        return a
    return a + b


def sub(a, b):
    if b is None:
        return a
    if a is None:
        return -b
    return a - b


def primitives(s):
    inv = 1.0 / s[0]
    u, v, w = s[1] * inv, s[2] * inv, s[3] * inv
    k = 0.5 * (u * u + v * v + w * w)
    p = 0.4 * (s[4] - s[0] * k)
    return u, v, w, k, p, (s[4] + p) * inv


def apply_jacobian(cell, sign, x):
    u, v, w, k, h = cell
    us = u + sign * DISS if sign else u
    q = sub(x[1], mul(u, x[0]))
    inner = sub(mul(k, x[0]), mul(u, x[1]))
    inner = sub(sub(inner, mul(v, x[2])), mul(w, x[3]))
    p = mul(0.4, add(inner, x[4]))
    top = x[1]
    if sign and x[0] is not None:
        top = add(top, mul(sign * DISS, x[0]))
    return [
        top,
        add(add(mul(us, x[1]), mul(u, q)), p),
        add(mul(v, q), mul(us, x[2])),
        add(mul(w, q), mul(us, x[3])),
        add(add(mul(h, q), mul(us, x[4])), mul(u, p)),
    ]


def jacobian_columns(cell, sign):
    u, v, w, k, h = cell
    shift = sign * DISS
    us = u + shift
    gk = 0.4 * k
    gv, gw = -0.4 * v, -0.4 * w
    return [
        [shift, gk - u * u, -(u * v), -(u * w), u * (gk - h)],
        [1.0, 1.6 * u + shift, v, w, h - 0.4 * (u * u)],
        [None, gv, us, None, u * gv],
        [None, gw, None, us, u * gw],
        [None, 0.4, None, None, 1.4 * u + shift],
    ]


def product(left, left_sign, right, right_sign):
    columns = [apply_jacobian(left, left_sign, c) for c in jacobian_columns(right, right_sign)]
    return [[columns[j][i] for j in range(5)] for i in range(5)]


def full(x):
    if x is None:
        return jnp.zeros((8, 128), F32)
    if isinstance(x, float):
        return jnp.full((8, 128), x, F32)
    return x


def dot_row(row, matrix, j):
    total = row[0] * matrix[0][j]
    for i in range(1, 5):
        total = total + row[i] * matrix[i][j]
    return total


def dot_vec(row, x):
    total = row[0] * x[0]
    for i in range(1, 5):
        total = total + row[i] * x[i]
    return total


def factor(matrix):
    d = [[matrix[i][j] for j in PIVOTS] for i in PIVOTS]
    inverse = []
    low = [[None] * 5 for _ in range(5)]
    for k in range(5):
        inverse.append(1.0 / d[k][k])
        for i in range(k + 1, 5):
            low[i][k] = d[i][k] * inverse[k]
            for j in range(k + 1, 5):
                d[i][j] = d[i][j] - low[i][k] * d[k][j]
    return d, low, inverse


def solve(factors, column):
    d, low, inverse = factors
    b = [column[i] for i in PIVOTS]
    for k in range(5):
        for i in range(k + 1, 5):
            b[i] = b[i] - low[i][k] * b[k]
    for k in reversed(range(5)):
        total = b[k]
        for j in range(k + 1, 5):
            total = total - d[k][j] * b[j]
        b[k] = total * inverse[k]
    x = [None] * 5
    for at, i in enumerate(PIVOTS):
        x[i] = b[at]
    return x


def quarters(c, lane):
    odd = (lane & 32) != 0
    high = (lane & 64) != 0

    def swap(a, b, mask, shift):
        return (
            jnp.where(mask, pltpu.roll(b, shift, 1), a),
            jnp.where(mask, b, pltpu.roll(a, 128 - shift, 1)),
        )

    c0, c1 = swap(c[0], c[1], odd, 32)
    c2, c3 = swap(c[2], c[3], odd, 32)
    c0, c2 = swap(c0, c2, high, 64)
    c1, c3 = swap(c1, c3, high, 64)
    return [c0, c1, c2, c3]


def pack(values, ref, rows, lane):
    values = list(values)
    while len(values) % 4:
        values.append(values[-1])
    for g in range(len(values) // 4):
        out = quarters(values[4 * g : 4 * g + 4], lane)
        for t in range(4):
            ref[pl.ds(8 * t * rows + g, 8, stride=rows), :] = out[t]


def unpack(ref, rows, count, lane):
    values = []
    for g in range((count + 3) // 4):
        got = [ref[pl.ds(8 * t * rows + g, 8, stride=rows), :] for t in range(4)]
        values += quarters(got, lane)
    return values[:count]


def kernel(
    state_ref, next_ref, diff_ref,
    st, pr, fx, rr, fac, left, halo_send, halo_left, halo_right,
    send_a, recv_a, send_b, recv_b, send_c, recv_c, sys, sol, xs, lin,
    ssem_h, rsem_h, ssem_a, rsem_a, ssem_b, rsem_b, ssem_c, rsem_c,
):
    me = lax.axis_index("stream")
    mine = lax.axis_index("span")

    barrier = pltpu.get_barrier_semaphore()

    def greet(d, _):
        pl.semaphore_signal(
            barrier, inc=1, device_id={"stream": lax.rem(me + d, N)}, device_id_type=MESH
        )
        return 0

    lax.fori_loop(1, N, greet, 0)
    span_right = lax.rem(mine + 1, SPAN)
    span_left = lax.rem(mine + SPAN - 1, SPAN)
    for other in (span_left, span_right):
        pl.semaphore_signal(barrier, inc=1, device_id={"span": other}, device_id_type=MESH)

    lane = lax.broadcasted_iota(jnp.int32, (8, 128), 1)
    sub_row = lax.broadcasted_iota(jnp.int32, (8, 128), 0)

    for f in range(5):
        for half in range(2):
            st[pl.ds(1 + 8 * half, 8), f] = jnp.swapaxes(
                state_ref[f, :, pl.ds(8 * half, 8), :], 0, 1
            )
    for f in range(5):
        packed = st[1, f]
        for i in range(CX):
            moved = pltpu.roll(st[1 + i, f], (2 + 4 * i) % 128, 1)
            packed = jnp.where((lane >> 2) == i, moved, packed)
        halo_send[f] = packed

    pl.semaphore_wait(barrier, N - 1 + 2)

    halos = []
    for at, (src, dst, who) in enumerate(
        (
            (st.at[CX], st.at[0], {"stream": lax.rem(me + 1, N)}),
            (st.at[1], st.at[CX + 1], {"stream": lax.rem(me + N - 1, N)}),
            (halo_send, halo_left, {"span": span_right}),
            (halo_send, halo_right, {"span": span_left}),
        )
    ):
        copy = pltpu.make_async_remote_copy(
            src_ref=src, dst_ref=dst, send_sem=ssem_h.at[at], recv_sem=rsem_h.at[at],
            device_id=who, device_id_type=MESH,
        )
        copy.start()
        halos.append(copy)

    def prepare(i, _):
        s = [st[i, f] for f in range(5)]
        u, v, w, k, p, h = primitives(s)
        for at, value in enumerate((u, v, w, k, h)):
            pr[i, at] = value
        flux = [s[1], s[1] * u + p, s[2] * u, s[3] * u, u * (s[4] + p)]
        for f in range(5):
            fx[i, f] = flux[f]
        return 0

    lax.fori_loop(1, CX + 1, prepare, 0)

    for copy in halos:
        copy.wait_recv()
    prepare(0, 0)
    prepare(CX + 1, 0)

    has_low = jnp.where(me > 0, 1.0, 0.0).astype(F32)
    has_high = jnp.where(me < N - 1, 1.0, 0.0).astype(F32)

    rim = [jnp.where((lane & 2) == 0, halo_left[f], halo_right[f]) for f in range(5)]
    _, v, _, _, p, _ = primitives(rim)
    rim_flux = [rim[2], rim[1] * v, rim[2] * v + p, rim[3] * v, v * (rim[4] + p)]
    for f in range(5):
        for i in range(CX):
            xs[1 + i, f] = pltpu.roll(rim_flux[f], (254 - 4 * i) % 128, 1)

    def right_side(i, _):
        s = [st[i, f] for f in range(5)]
        u, v, w, k, h = (pr[i, at] for at in range(5))
        total = h * s[0]
        p = total - s[4]
        g = [s[2], s[1] * v, s[2] * v + p, s[3] * v, v * total]
        wall = [s[3], s[1] * w, s[2] * w, s[3] * w + p, w * total]
        low = jnp.where(i == 1, has_low, 1.0)
        high = jnp.where(i == CX, has_high, 1.0)
        for f in range(5):
            edge = xs[i, f]
            near = pltpu.roll(jnp.where(lane < 1, edge, g[f]), 127, 1) - pltpu.roll(
                jnp.where(lane >= 127, edge, g[f]), 1, 1
            )
            far = pltpu.roll(jnp.where(lane < 2, edge, g[f]), 126, 1) - pltpu.roll(
                jnp.where(lane >= 126, edge, g[f]), 2, 1
            )
            span = 8.0 * near - far
            mirrored = wall[f] if f == 3 else -wall[f]
            above = jnp.where(sub_row == 7, wall[f], pltpu.roll(wall[f], 7, 0))
            below = jnp.where(sub_row == 0, mirrored, pltpu.roll(wall[f], 1, 0))
            stream = fx[i + 1, f] * high - fx[i - 1, f] * low
            curve = st[i + 1, f] * high + st[i - 1, f] * low - 2.0 * s[f]
            rr[i, f] = (
                DISS * curve - stream - (1.0 / 384.0) * span - (1.0 / 64.0) * (above - below)
            )
        return 0

    lax.fori_loop(1, CX + 1, right_side, 0)

    def cell(i):
        return tuple(pr[i, at] for at in range(5))

    def source(i):
        return [rr[i, f] for f in range(5)]

    zero = jnp.zeros((8, 128), F32)
    one = jnp.ones((8, 128), F32)
    for i in range(5):
        for j in range(5):
            fac[0, 5 * i + j] = zero
            fac[0, 25 + 5 * i + j] = one if i == j else zero
        fac[0, 50 + i] = zero

    def eliminate(m, _):
        i = 2 * m + 2
        below2, below1, here, above1, above2 = (cell(i + t) for t in range(-2, 3))
        low = [[full(x) for x in row] for row in product(below1, 1.0, below2, 1.0)]
        upper = [[full(x) for x in row] for row in product(above1, -1.0, above2, -1.0)]
        first = product(below1, 1.0, here, -1.0)
        second = product(above1, -1.0, here, 1.0)
        r_low = apply_jacobian(below1, 1.0, source(i - 1))
        r_high = apply_jacobian(above1, -1.0, source(i + 1))
        r_here = source(i)
        f_before = [[fac[m, 5 * a + b] for b in range(5)] for a in range(5)]
        y_before = [fac[m, 50 + a] for a in range(5)]
        diag = []
        for a in range(5):
            row = []
            for b in range(5):
                value = full(add(first[a][b], second[a][b])) - dot_row(low[a], f_before, b)
                row.append(value + DIAG if a == b else value)
            diag.append(row)
        factors = factor(diag)
        column = [
            (1.0 / 25.6) * r_here[a] + (r_low[a] - r_high[a]) + dot_vec(low[a], y_before)
            for a in range(5)
        ]
        y = solve(factors, column)
        for a in range(5):
            fac[m + 1, 50 + a] = y[a]
        for b in range(5):
            x = solve(factors, [upper[a][b] for a in range(5)])
            for a in range(5):
                fac[m + 1, 5 * a + b] = x[a]
        s_before = [[fac[m, 25 + 5 * a + b] for b in range(5)] for a in range(5)]
        for b in range(5):
            x = solve(factors, [dot_row(low[a], s_before, b) for a in range(5)])
            for a in range(5):
                fac[m + 1, 25 + 5 * a + b] = x[a]
        return 0

    lax.fori_loop(0, 7, eliminate, 0)

    below2, below1, here = cell(CX - 2), cell(CX - 1), cell(CX)
    low = [[full(x) for x in row] for row in product(below1, 1.0, below2, 1.0)]
    own = product(below1, 1.0, here, -1.0)
    r_low = apply_jacobian(below1, 1.0, source(CX - 1))
    r_here = source(CX)
    f_last = [[fac[7, 5 * a + b] for b in range(5)] for a in range(5)]
    s_last = [[fac[7, 25 + 5 * a + b] for b in range(5)] for a in range(5)]
    y_last = [fac[7, 50 + a] for a in range(5)]
    to_low = [dot_row(low[a], s_last, b) for a in range(5) for b in range(5)]
    to_own = []
    for a in range(5):
        for b in range(5):
            value = full(own[a][b]) - dot_row(low[a], f_last, b)
            to_own.append(value + DIAG if a == b else value)
    to_source = [(1.0 / 25.6) * r_here[a] + r_low[a] + dot_vec(low[a], y_last) for a in range(5)]
    pack(to_low + to_own + to_source, send_a, ROWS, lane)

    def exchange(send, recv, ssem, rsem, rows):
        def copy_to(d):
            other = lax.rem(me + d, N)
            return pltpu.make_async_remote_copy(
                src_ref=send.at[pl.ds(pl.multiple_of(other * rows, rows), rows)],
                dst_ref=recv.at[pl.ds(pl.multiple_of(me * rows, rows), rows)],
                send_sem=ssem.at[d], recv_sem=rsem.at[d],
                device_id={"stream": other}, device_id_type=MESH,
            )

        def copy_from(d):
            other = lax.rem(me + N - d, N)
            return pltpu.make_async_remote_copy(
                src_ref=send.at[pl.ds(pl.multiple_of(me * rows, rows), rows)],
                dst_ref=recv.at[pl.ds(pl.multiple_of(other * rows, rows), rows)],
                send_sem=ssem.at[d], recv_sem=rsem.at[d],
                device_id={"stream": other}, device_id_type=MESH,
            )

        def start():
            def body(d, _):
                copy_to(d).start()
                return 0

            lax.fori_loop(1, N, body, 0)
            place = pl.ds(pl.multiple_of(me * rows, rows), rows)
            recv[place, :] = send[place, :]

        def wait_recv():
            def body(d, _):
                copy_from(d).wait_recv()
                return 0

            lax.fori_loop(1, N, body, 0)

        def wait_send():
            def body(d, _):
                copy_to(d).wait_send()
                return 0

            lax.fori_loop(1, N, body, 0)

        return start, wait_recv, wait_send

    start_a, arrived_a, sent_a = exchange(send_a, recv_a, ssem_a, rsem_a, ROWS)
    start_b, arrived_b, sent_b = exchange(send_b, recv_b, ssem_b, rsem_b, ROWS)
    start_c, arrived_c, sent_c = exchange(send_c, recv_c, ssem_c, rsem_c, BACK_ROWS)
    start_a()

    for copy in halos:
        copy.wait_send()

    outer, first, second = cell(0), cell(1), cell(2)
    diag = product(first, -1.0, outer, 1.0)
    upper = product(first, -1.0, second, -1.0)
    r_first = apply_jacobian(first, -1.0, source(1))
    for a in range(5):
        for b in range(5):
            left[5 * a + b] = full(upper[a][b])
            left[25 + 5 * a + b] = full(diag[a][b])
        left[50 + a] = -r_first[a]

    def follow(m, _):
        f_here = [[fac[m, 5 * a + b] for b in range(5)] for a in range(5)]
        s_here = [[fac[m, 25 + 5 * a + b] for b in range(5)] for a in range(5)]
        y_here = [fac[m, 50 + a] for a in range(5)]
        for a in range(5):
            row = [left[5 * a + b] for b in range(5)]
            for b in range(5):
                left[25 + 5 * a + b] = left[25 + 5 * a + b] - dot_row(row, s_here, b)
                left[5 * a + b] = dot_row(row, f_here, b)
            left[50 + a] = left[50 + a] + dot_vec(row, y_here)
        return 0

    lax.fori_loop(1, 8, follow, 0)
    pack([left[at] for at in range(55)], send_b, ROWS, lane)
    start_b()

    arrived_a()
    at_first = (sub_row == 0) & (lane < 32)
    at_last = (sub_row == 7) & (lane >= 96)
    values = unpack(recv_a, ROWS, 55, lane)
    for at in range(25):
        sys[at] = jnp.where(at_first, 0.0, values[at])
        sys[25 + at] = values[25 + at]
    for a in range(5):
        sys[75 + a] = values[50 + a]
    arrived_b()

    def after(x, d):
        if d >= 8:
            return pltpu.roll(x, 128 - 4 * d, 1)
        x = pltpu.roll(x, 8 - d, 0)
        return jnp.where(sub_row >= 8 - d, pltpu.roll(x, 96, 1), x)

    def before(x, d):
        if d >= 8:
            return pltpu.roll(x, 4 * d, 1)
        x = pltpu.roll(x, d, 0)
        return jnp.where(sub_row < d, pltpu.roll(x, 32, 1), x)

    values = unpack(recv_b, ROWS, 55, lane)
    values = [jnp.where(at_last, 0.0, after(x, 1)) for x in values]
    for at in range(25):
        sys[50 + at] = values[at]
        sys[25 + at] = sys[25 + at] + values[25 + at]
    for a in range(5):
        sys[75 + a] = sys[75 + a] + values[50 + a]

    for level in range(5):
        d = 1 << level
        factors = factor([[sys[25 + 5 * a + b] for b in range(5)] for a in range(5)])
        for b in range(5):
            x = solve(factors, [sys[5 * a + b] for a in range(5)])
            for a in range(5):
                sol[5 * a + b] = x[a]
            x = solve(factors, [sys[50 + 5 * a + b] for a in range(5)])
            for a in range(5):
                sol[25 + 5 * a + b] = x[a]
        x = solve(factors, [sys[75 + a] for a in range(5)])
        for a in range(5):
            sol[50 + a] = x[a]
        lows = [[sol[5 * a + b] for b in range(5)] for a in range(5)]
        ups = [[sol[25 + 5 * a + b] for b in range(5)] for a in range(5)]
        for b in range(5):
            low_column = [[before(sol[5 * a + b], d)] for a in range(5)]
            up_column = [[after(sol[25 + 5 * a + b], d)] for a in range(5)]
            cross_low = [[before(sol[25 + 5 * a + b], d)] for a in range(5)]
            cross_up = [[after(sol[5 * a + b], d)] for a in range(5)]
            for a in range(5):
                value = -(dot_row(lows[a], cross_low, 0) + dot_row(ups[a], cross_up, 0))
                sys[25 + 5 * a + b] = value + 1.0 if a == b else value
                if level < 4:
                    sys[5 * a + b] = dot_row(lows[a], low_column, 0)
                    sys[50 + 5 * a + b] = dot_row(ups[a], up_column, 0)
        r_low = [before(sol[50 + a], d) for a in range(5)]
        r_high = [after(sol[50 + a], d) for a in range(5)]
        for a in range(5):
            sys[75 + a] = sol[50 + a] + dot_vec(lows[a], r_low) + dot_vec(ups[a], r_high)
    factors = factor([[sys[25 + 5 * a + b] for b in range(5)] for a in range(5)])
    ends = solve(factors, [sys[75 + a] for a in range(5)])
    starts = [jnp.where(at_first, 0.0, before(x, 1)) for x in ends]
    pack(ends + starts, send_c, BACK_ROWS, lane)
    start_c()
    arrived_c()
    values = unpack(recv_c, BACK_ROWS, 10, lane)
    for f in range(5):
        xs[CX, f] = values[f]
        xs[0, f] = values[5 + f]

    def back(t, _):
        m = 7 - t
        x_left = [xs[0, f] for f in range(5)]
        x_right = [xs[2 * m + 2, f] for f in range(5)]
        for a in range(5):
            row_f = [fac[m, 5 * a + b] for b in range(5)]
            row_s = [fac[m, 25 + 5 * a + b] for b in range(5)]
            xs[2 * m, a] = fac[m, 50 + a] + (dot_vec(row_s, x_left) + dot_vec(row_f, x_right))
        return 0

    lax.fori_loop(0, 7, back, 0)

    def even(t, _):
        i = 2 * t + 1
        low_part = apply_jacobian(cell(i - 1), 1.0, [xs[i - 1, f] for f in range(5)])
        high_part = apply_jacobian(cell(i + 1), -1.0, [xs[i + 1, f] for f in range(5)])
        for f in range(5):
            xs[i, f] = 25.6 * (rr[i, f] + (low_part[f] - high_part[f]))
        return 0

    lax.fori_loop(0, 8, even, 0)

    def advance(i, _):
        new = [st[i, f] + xs[i, f] for f in range(5)]
        flux = apply_jacobian(cell(i), 0.0, new)
        for f in range(5):
            st[i, f] = new[f]
            lin[i, f] = flux[f]
        return 0

    held = apply_jacobian(cell(CX - 1), 1.0, [xs[CX - 1, f] for f in range(5)])
    t = [rr[CX, f] + held[f] - (1.25 / 32.0) * xs[CX, f] for f in range(5)]
    u, v, w, k, h = cell(CX + 1)
    z = u - DISS
    z_inv = 1.0 / z
    p0 = t[1] - (z + u) * t[0]
    x2 = (t[2] - v * t[0]) * z_inv
    x3 = (t[3] - w * t[0]) * z_inv
    x4 = (t[4] - h * t[0] - u * p0) * z_inv
    x0 = (p0 - 0.4 * (x4 - u * t[0] - v * x2 - w * x3)) / (0.4 * (h - k) - z * z)
    beyond = [x0, t[0] + DISS * x0, x2 + v * x0, x3 + w * x0, x4 + (h - u * z) * x0]
    base = apply_jacobian(cell(CX + 1), 0.0, [st[CX + 1, f] for f in range(5)])
    for f in range(5):
        lin[CX + 1, f] = has_high * (base[f] + (t[f] + DISS * beyond[f]))
    lax.fori_loop(0, CX + 1, advance, 0)
    for f in range(5):
        lin[0, f] = has_low * lin[0, f]

    def differ(i, _):
        for f in range(5):
            xs[i, f] = -0.5 * (lin[i + 1, f] - lin[i - 1, f])
        return 0

    lax.fori_loop(1, CX + 1, differ, 0)
    for f in range(5):
        for half in range(2):
            place = pl.ds(8 * half, 8)
            next_ref[f, :, place, :] = jnp.swapaxes(st[pl.ds(1 + 8 * half, 8), f], 0, 1)
            diff_ref[f, :, place, :] = jnp.swapaxes(xs[pl.ds(1 + 8 * half, 8), f], 0, 1)

    sent_a()
    sent_b()
    sent_c()


def on_device(state):
    def cells(*shape):
        return pltpu.VMEM(shape + (8, 128), F32)

    return pl.pallas_call(
        kernel,
        out_shape=(jax.ShapeDtypeStruct(state.shape, F32), jax.ShapeDtypeStruct(state.shape, F32)),
        in_specs=[pl.BlockSpec(memory_space=pltpu.VMEM)],
        out_specs=(pl.BlockSpec(memory_space=pltpu.VMEM), pl.BlockSpec(memory_space=pltpu.VMEM)),
        scratch_shapes=[
            cells(CX + 2, 5), cells(CX + 2, 5), cells(CX + 2, 5), cells(CX + 2, 5),
            cells(8, 55), cells(55), cells(5), cells(5), cells(5),
            pltpu.VMEM((N * ROWS, 128), F32), pltpu.VMEM((N * ROWS, 128), F32),
            pltpu.VMEM((N * ROWS, 128), F32), pltpu.VMEM((N * ROWS, 128), F32),
            pltpu.VMEM((N * BACK_ROWS, 128), F32), pltpu.VMEM((N * BACK_ROWS, 128), F32),
            cells(80), cells(55), cells(CX + 2, 5), cells(CX + 2, 5),
            pltpu.SemaphoreType.DMA((4,)), pltpu.SemaphoreType.DMA((4,)),
            pltpu.SemaphoreType.DMA((N,)), pltpu.SemaphoreType.DMA((N,)),
            pltpu.SemaphoreType.DMA((N,)), pltpu.SemaphoreType.DMA((N,)),
            pltpu.SemaphoreType.DMA((N,)), pltpu.SemaphoreType.DMA((N,)),
        ],
        compiler_params=pltpu.CompilerParams(
            collective_id=0, has_side_effects=True, vmem_limit_bytes=32 * 1024 * 1024
        ),
    )(state)


def solution(mesh):
    spec = P(None, None, "stream", "span")
    return jax.shard_map(
        on_device, mesh=mesh, in_specs=(spec,), out_specs=(spec, spec), check_vma=False
    )
```

profile of v0, /device:TPU:8, one launch (start us, length us, event | category | flops | bytes accessed | tf_op | source)
XLA Modules:
  0.0 47.1 jit_solution(8062246343710313184)
XLA Ops:
  0.6 0.0 copy-start
  0.6 1.0 %copy-done = f32[5,8,16,128]{3,2,1,0:T(8,128)S(1)} copy-done((f32[5,8,16,128]{3,2,1,0:T(8,128)S(1)}, f32[5,8,16,128]{3,2,1,0:T(8,128)}, u32[]{:S(2)}) %copy-start) | copy-done | bytes 327704
  1.6 44.0 %shard_map.30 = (f32[5,8,16,128]{3,2,1,0:T(8,128)S(1)}, f32[5,8,16,128]{3,2,1,0:T(8,128)S(1)}) custom-call(f32[5,8,16,128]{3,2,1,0:T(8,128)S(1)} %copy-done), custom_call_target="tpu_custom_call" | custom-call | tf_op jit(solution)/shard_map/pallas_call | solution.py:583
  45.7 0.7 %copy.5 = f32[5,8,16,128]{3,2,1,0:T(8,128)} copy(f32[5,8,16,128]{3,2,1,0:T(8,128)S(1)} %get-tuple-element.4) | data formatting | bytes 655360
  46.4 0.7 %copy.6 = f32[5,8,16,128]{3,2,1,0:T(8,128)} copy(f32[5,8,16,128]{3,2,1,0:T(8,128)S(1)} %get-tuple-element.5) | data formatting | bytes 655360
Async XLA Ops:
  0.6 1.0 %copy-start = (f32[5,8,16,128]{3,2,1,0:T(8,128)S(1)}, f32[5,8,16,128]{3,2,1,0:T(8,128)}, u32[]{:S(2)}) copy-start(f32[5,8,16,128]{3,2,1,0:T(8,128)} %state_ref.1) | copy-start | bytes 983044
where the time goes:
time: 47.2 us; the launch traced here: 47.1 us
  Pallas kernels  44 us (93%)
  local copies, waits for them, and re-layouts  2.42 us (5%)
  between operations  0.65 us (1%)
    pallas_call x1, Pallas kernels, on_device(): pl.pallas_call(kernel, out_shape=(jax.ShapeDtypeStruct(state.shape, F32),...  44 us
    unnamed x4, local copies, waits for them, and re-layouts  2.42 us

commit v1 on v0

--- a/solution.py
+++ b/solution.py
@@ -12,8 +12,9 @@
 DISS = 1.0 / 256.0
 DIAG = 1.25 / 819.2
 PIVOTS = (1, 2, 3, 0, 4)
-ROWS = 16
-BACK_ROWS = 8
+MATRIX = (27, 32)
+SOURCE = (3, 8)
+BACK = (3, 8)
 F32 = jnp.float32
 
 
@@ -98,6 +99,20 @@
     return x
 
 
+def times_jacobian(t, cell):
+    u, v, w, k, h = cell
+    us = u + DISS
+    alpha = (t[1] * u + t[2] * v) + (t[3] * w + t[4] * h)
+    beta = 0.4 * (t[1] + u * t[4])
+    return [
+        (beta * k - u * alpha) + DISS * t[0],
+        (t[0] + us * t[1]) + (alpha - beta * u),
+        us * t[2] - beta * v,
+        us * t[3] - beta * w,
+        us * t[4] + beta,
+    ]
+
+
 def dot_row(row, matrix, j):
     total = row[0] * matrix[0][j]
     for i in range(1, 5):
@@ -123,6 +138,25 @@
             for j in range(k + 1, 5):
                 d[i][j] = d[i][j] - low[i][k] * d[k][j]
     return d, low, inverse
+
+
+def keep_factors(factors, ref, m):
+    d, low, inverse = factors
+    kept = [d[k][j] for k in range(5) for j in range(k + 1, 5)]
+    kept += [low[i][k] for k in range(5) for i in range(k + 1, 5)] + inverse
+    for at, value in enumerate(kept):
+        ref[m, at] = value
+
+
+def kept_factors(ref, m):
+    d, low = [[None] * 5 for _ in range(5)], [[None] * 5 for _ in range(5)]
+    at = 0
+    for k in range(5):
+        for j in range(k + 1, 5):
+            d[k][j] = ref[m, at]
+            low[j][k] = ref[m, at + 10]
+            at += 1
+    return d, low, [ref[m, 20 + k] for k in range(5)]
 
 
 def solve(factors, column):
@@ -159,18 +193,20 @@
     return [c0, c1, c2, c3]
 
 
-def pack(values, ref, rows, lane):
+def pack(values, ref, rows, lane, first=0):
     values = list(values)
+    rows = rows[1]
     while len(values) % 4:
         values.append(values[-1])
     for g in range(len(values) // 4):
         out = quarters(values[4 * g : 4 * g + 4], lane)
         for t in range(4):
-            ref[pl.ds(8 * t * rows + g, 8, stride=rows), :] = out[t]
+            ref[pl.ds(8 * t * rows + first + g, 8, stride=rows), :] = out[t]
 
 
 def unpack(ref, rows, count, lane):
     values = []
+    rows = rows[1]
     for g in range((count + 3) // 4):
         got = [ref[pl.ds(8 * t * rows + g, 8, stride=rows), :] for t in range(4)]
         values += quarters(got, lane)
@@ -179,14 +215,20 @@
 
 def kernel(
     state_ref, next_ref, diff_ref,
-    st, pr, fx, rr, fac, left, halo_send, halo_left, halo_right,
+    here, st, pr, fx, rr, fac, ys, fct, lows, left, halo_send, halo_left, halo_right,
     send_a, recv_a, send_b, recv_b, send_c, recv_c, sys, sol, xs, lin,
-    ssem_h, rsem_h, ssem_a, rsem_a, ssem_b, rsem_b, ssem_c, rsem_c,
+    sem_in, ssem_h, rsem_h, ssem_x, rsem_x,
 ):
     me = lax.axis_index("stream")
     mine = lax.axis_index("span")
+    span_right = lax.rem(mine + 1, SPAN)
+    span_left = lax.rem(mine + SPAN - 1, SPAN)
 
     barrier = pltpu.get_barrier_semaphore()
+    load = pltpu.make_async_copy(state_ref, here, sem_in)
+    load.start()
+    for other in (span_left, span_right):
+        pl.semaphore_signal(barrier, inc=1, device_id={"span": other}, device_id_type=MESH)
 
     def greet(d, _):
         pl.semaphore_signal(
@@ -195,19 +237,104 @@
         return 0
 
     lax.fori_loop(1, N, greet, 0)
-    span_right = lax.rem(mine + 1, SPAN)
-    span_left = lax.rem(mine + SPAN - 1, SPAN)
-    for other in (span_left, span_right):
-        pl.semaphore_signal(barrier, inc=1, device_id={"span": other}, device_id_type=MESH)
+    load.wait()
 
     lane = lax.broadcasted_iota(jnp.int32, (8, 128), 1)
     sub_row = lax.broadcasted_iota(jnp.int32, (8, 128), 0)
 
     for f in range(5):
         for half in range(2):
-            st[pl.ds(1 + 8 * half, 8), f] = jnp.swapaxes(
-                state_ref[f, :, pl.ds(8 * half, 8), :], 0, 1
-            )
+            st[pl.ds(1 + 8 * half, 8), f] = jnp.swapaxes(here[f, :, pl.ds(8 * half, 8), :], 0, 1)
+
+    def prepare(i, _):
+        s = [st[i, f] for f in range(5)]
+        u, v, w, k, p, h = primitives(s)
+        for at, value in enumerate((u, v, w, k, h)):
+            pr[i, at] = value
+        flux = [s[1], s[1] * u + p, s[2] * u, s[3] * u, u * (s[4] + p)]
+        for f in range(5):
+            fx[i, f] = flux[f]
+        return 0
+
+    lax.fori_loop(1, CX + 1, prepare, 0)
+
+    def cell(i):
+        return tuple(pr[i, at] for at in range(5))
+
+    def eliminate(m, first_node):
+        i = 2 * m + 2
+        below1, middle, above1, above2 = (cell(i + t) for t in range(-1, 3))
+        upper = [[full(x) for x in row] for row in product(above1, -1.0, above2, -1.0)]
+        first = product(below1, 1.0, middle, -1.0)
+        second = product(above1, -1.0, middle, 1.0)
+        diag = [[full(add(first[a][b], second[a][b])) for b in range(5)] for a in range(5)]
+        if first_node:
+            columns = jacobian_columns(below1, 1.0)
+            spike = [[full(columns[b][a]) for b in range(5)] for a in range(5)]
+        else:
+            low = [[full(x) for x in row] for row in product(below1, 1.0, cell(i - 2), 1.0)]
+            f_before = [[fac[m - 1, 5 * a + b] for b in range(5)] for a in range(5)]
+            for a in range(5):
+                for b in range(5):
+                    lows[m, 5 * a + b] = low[a][b]
+                    diag[a][b] = diag[a][b] - dot_row(low[a], f_before, b)
+        for a in range(5):
+            diag[a][a] = diag[a][a] + DIAG
+        factors = factor(diag)
+        keep_factors(factors, fct, m)
+        for b in range(5):
+            x = solve(factors, [upper[a][b] for a in range(5)])
+            for a in range(5):
+                fac[m, 5 * a + b] = x[a]
+        if not first_node:
+            s_before = [[fac[m - 1, 25 + 5 * a + b] for b in range(5)] for a in range(5)]
+            spike = [[dot_row(low[a], s_before, b) for b in range(5)] for a in range(5)]
+        for b in range(5):
+            x = solve(factors, [spike[a][b] for a in range(5)])
+            for a in range(5):
+                fac[m, 25 + 5 * a + b] = x[a]
+
+    def eliminate_step(m, _):
+        eliminate(m, False)
+        return 0
+
+    eliminate(0, True)
+    lax.fori_loop(1, 7, eliminate_step, 0)
+
+    low = [[full(x) for x in row] for row in product(cell(CX - 1), 1.0, cell(CX - 2), 1.0)]
+    own = product(cell(CX - 1), 1.0, cell(CX), -1.0)
+    f_last = [[fac[6, 5 * a + b] for b in range(5)] for a in range(5)]
+    s_last = [[fac[6, 25 + 5 * a + b] for b in range(5)] for a in range(5)]
+    to_low = [dot_row(low[a], s_last, b) for a in range(5) for b in range(5)]
+    to_own = []
+    for a in range(5):
+        for b in range(5):
+            lows[7, 5 * a + b] = low[a][b]
+            value = full(own[a][b]) - dot_row(low[a], f_last, b)
+            to_own.append(value + DIAG if a == b else value)
+    pack((to_low + to_own)[:48], send_a, MATRIX, lane)
+
+    upper = product(cell(1), -1.0, cell(2), -1.0)
+    columns = jacobian_columns(cell(1), -1.0)
+    for a in range(5):
+        for b in range(5):
+            left[0, 5 * a + b] = full(upper[a][b])
+            left[0, 25 + 5 * a + b] = full(columns[b][a])
+
+    def follow(m, _):
+        f_here = [[fac[m, 5 * a + b] for b in range(5)] for a in range(5)]
+        s_here = [[fac[m, 25 + 5 * a + b] for b in range(5)] for a in range(5)]
+        for a in range(5):
+            row = [left[m, 5 * a + b] for b in range(5)]
+            for b in range(5):
+                left[m + 1, 25 + 5 * a + b] = left[m, 25 + 5 * a + b] - dot_row(row, s_here, b)
+                left[m + 1, 5 * a + b] = dot_row(row, f_here, b)
+        return 0
+
+    lax.fori_loop(0, 7, follow, 0)
+    rest = to_own[-2:] + [left[7, at] for at in range(50)] + list(cell(CX))
+    pack(rest, send_a, MATRIX, lane, 12)
+
     for f in range(5):
         packed = st[1, f]
         for i in range(CX):
@@ -233,17 +360,36 @@
         copy.start()
         halos.append(copy)
 
-    def prepare(i, _):
-        s = [st[i, f] for f in range(5)]
-        u, v, w, k, p, h = primitives(s)
-        for at, value in enumerate((u, v, w, k, h)):
-            pr[i, at] = value
-        flux = [s[1], s[1] * u + p, s[2] * u, s[3] * u, u * (s[4] + p)]
-        for f in range(5):
-            fx[i, f] = flux[f]
-        return 0
-
-    lax.fori_loop(1, CX + 1, prepare, 0)
+    def exchange(send, recv, at, rows):
+        count, stride = rows
+
+        def start():
+            def body(d, _):
+                other = lax.rem(me + d, N)
+                pltpu.make_async_remote_copy(
+                    src_ref=send.at[pl.ds(pl.multiple_of(other * stride, 8), count)],
+                    dst_ref=recv.at[pl.ds(pl.multiple_of(me * stride, 8), count)],
+                    send_sem=ssem_x.at[at], recv_sem=rsem_x.at[at],
+                    device_id={"stream": other}, device_id_type=MESH,
+                ).start()
+                return 0
+
+            lax.fori_loop(1, N, body, 0)
+            place = pl.ds(pl.multiple_of(me * stride, 8), stride)
+            recv[place, :] = send[place, :]
+
+        everything = pltpu.make_async_remote_copy(
+            src_ref=send.at[pl.ds(0, (N - 1) * count)],
+            dst_ref=recv.at[pl.ds(0, (N - 1) * count)],
+            send_sem=ssem_x.at[at], recv_sem=rsem_x.at[at],
+            device_id={"stream": lax.rem(me + 1, N)}, device_id_type=MESH,
+        )
+        return start, everything.wait_recv, everything.wait_send
+
+    start_a, arrived_a, sent_a = exchange(send_a, recv_a, 0, MATRIX)
+    start_b, arrived_b, sent_b = exchange(send_b, recv_b, 1, SOURCE)
+    start_c, arrived_c, sent_c = exchange(send_c, recv_c, 2, BACK)
+    start_a()
 
     for copy in halos:
         copy.wait_recv()
@@ -290,165 +436,35 @@
 
     lax.fori_loop(1, CX + 1, right_side, 0)
 
-    def cell(i):
-        return tuple(pr[i, at] for at in range(5))
-
     def source(i):
         return [rr[i, f] for f in range(5)]
 
-    zero = jnp.zeros((8, 128), F32)
-    one = jnp.ones((8, 128), F32)
-    for i in range(5):
-        for j in range(5):
-            fac[0, 5 * i + j] = zero
-            fac[0, 25 + 5 * i + j] = one if i == j else zero
-        fac[0, 50 + i] = zero
-
-    def eliminate(m, _):
+    y = None
+    r_first = apply_jacobian(cell(1), -1.0, source(1))
+    to_left = [-r_first[a] for a in range(5)]
+    for m in range(8):
         i = 2 * m + 2
-        below2, below1, here, above1, above2 = (cell(i + t) for t in range(-2, 3))
-        low = [[full(x) for x in row] for row in product(below1, 1.0, below2, 1.0)]
-        upper = [[full(x) for x in row] for row in product(above1, -1.0, above2, -1.0)]
-        first = product(below1, 1.0, here, -1.0)
-        second = product(above1, -1.0, here, 1.0)
-        r_low = apply_jacobian(below1, 1.0, source(i - 1))
-        r_high = apply_jacobian(above1, -1.0, source(i + 1))
         r_here = source(i)
-        f_before = [[fac[m, 5 * a + b] for b in range(5)] for a in range(5)]
-        y_before = [fac[m, 50 + a] for a in range(5)]
-        diag = []
-        for a in range(5):
-            row = []
-            for b in range(5):
-                value = full(add(first[a][b], second[a][b])) - dot_row(low[a], f_before, b)
-                row.append(value + DIAG if a == b else value)
-            diag.append(row)
-        factors = factor(diag)
-        column = [
-            (1.0 / 25.6) * r_here[a] + (r_low[a] - r_high[a]) + dot_vec(low[a], y_before)
-            for a in range(5)
-        ]
-        y = solve(factors, column)
-        for a in range(5):
-            fac[m + 1, 50 + a] = y[a]
-        for b in range(5):
-            x = solve(factors, [upper[a][b] for a in range(5)])
+        r_low = apply_jacobian(cell(i - 1), 1.0, source(i - 1))
+        column = [(1.0 / 25.6) * r_here[a] + r_low[a] for a in range(5)]
+        if m < 7:
+            r_high = apply_jacobian(cell(i + 1), -1.0, source(i + 1))
+            column = [column[a] - r_high[a] for a in range(5)]
+        if m > 0:
+            column = [
+                column[a] + dot_vec([lows[m, 5 * a + b] for b in range(5)], y) for a in range(5)
+            ]
+        if m < 7:
+            y = solve(kept_factors(fct, m), column)
             for a in range(5):
-                fac[m + 1, 5 * a + b] = x[a]
-        s_before = [[fac[m, 25 + 5 * a + b] for b in range(5)] for a in range(5)]
-        for b in range(5):
-            x = solve(factors, [dot_row(low[a], s_before, b) for a in range(5)])
-            for a in range(5):
-                fac[m + 1, 25 + 5 * a + b] = x[a]
-        return 0
-
-    lax.fori_loop(0, 7, eliminate, 0)
-
-    below2, below1, here = cell(CX - 2), cell(CX - 1), cell(CX)
-    low = [[full(x) for x in row] for row in product(below1, 1.0, below2, 1.0)]
-    own = product(below1, 1.0, here, -1.0)
-    r_low = apply_jacobian(below1, 1.0, source(CX - 1))
-    r_here = source(CX)
-    f_last = [[fac[7, 5 * a + b] for b in range(5)] for a in range(5)]
-    s_last = [[fac[7, 25 + 5 * a + b] for b in range(5)] for a in range(5)]
-    y_last = [fac[7, 50 + a] for a in range(5)]
-    to_low = [dot_row(low[a], s_last, b) for a in range(5) for b in range(5)]
-    to_own = []
-    for a in range(5):
-        for b in range(5):
-            value = full(own[a][b]) - dot_row(low[a], f_last, b)
-            to_own.append(value + DIAG if a == b else value)
-    to_source = [(1.0 / 25.6) * r_here[a] + r_low[a] + dot_vec(low[a], y_last) for a in range(5)]
-    pack(to_low + to_own + to_source, send_a, ROWS, lane)
-
-    def exchange(send, recv, ssem, rsem, rows):
-        def copy_to(d):
-            other = lax.rem(me + d, N)
-            return pltpu.make_async_remote_copy(
-                src_ref=send.at[pl.ds(pl.multiple_of(other * rows, rows), rows)],
-                dst_ref=recv.at[pl.ds(pl.multiple_of(me * rows, rows), rows)],
-                send_sem=ssem.at[d], recv_sem=rsem.at[d],
-                device_id={"stream": other}, device_id_type=MESH,
-            )
-
-        def copy_from(d):
-            other = lax.rem(me + N - d, N)
-            return pltpu.make_async_remote_copy(
-                src_ref=send.at[pl.ds(pl.multiple_of(me * rows, rows), rows)],
-                dst_ref=recv.at[pl.ds(pl.multiple_of(other * rows, rows), rows)],
-                send_sem=ssem.at[d], recv_sem=rsem.at[d],
-                device_id={"stream": other}, device_id_type=MESH,
-            )
-
-        def start():
-            def body(d, _):
-                copy_to(d).start()
-                return 0
-
-            lax.fori_loop(1, N, body, 0)
-            place = pl.ds(pl.multiple_of(me * rows, rows), rows)
-            recv[place, :] = send[place, :]
-
-        def wait_recv():
-            def body(d, _):
-                copy_from(d).wait_recv()
-                return 0
-
-            lax.fori_loop(1, N, body, 0)
-
-        def wait_send():
-            def body(d, _):
-                copy_to(d).wait_send()
-                return 0
-
-            lax.fori_loop(1, N, body, 0)
-
-        return start, wait_recv, wait_send
-
-    start_a, arrived_a, sent_a = exchange(send_a, recv_a, ssem_a, rsem_a, ROWS)
-    start_b, arrived_b, sent_b = exchange(send_b, recv_b, ssem_b, rsem_b, ROWS)
-    start_c, arrived_c, sent_c = exchange(send_c, recv_c, ssem_c, rsem_c, BACK_ROWS)
-    start_a()
-
-    for copy in halos:
-        copy.wait_send()
-
-    outer, first, second = cell(0), cell(1), cell(2)
-    diag = product(first, -1.0, outer, 1.0)
-    upper = product(first, -1.0, second, -1.0)
-    r_first = apply_jacobian(first, -1.0, source(1))
-    for a in range(5):
-        for b in range(5):
-            left[5 * a + b] = full(upper[a][b])
-            left[25 + 5 * a + b] = full(diag[a][b])
-        left[50 + a] = -r_first[a]
-
-    def follow(m, _):
-        f_here = [[fac[m, 5 * a + b] for b in range(5)] for a in range(5)]
-        s_here = [[fac[m, 25 + 5 * a + b] for b in range(5)] for a in range(5)]
-        y_here = [fac[m, 50 + a] for a in range(5)]
-        for a in range(5):
-            row = [left[5 * a + b] for b in range(5)]
-            for b in range(5):
-                left[25 + 5 * a + b] = left[25 + 5 * a + b] - dot_row(row, s_here, b)
-                left[5 * a + b] = dot_row(row, f_here, b)
-            left[50 + a] = left[50 + a] + dot_vec(row, y_here)
-        return 0
-
-    lax.fori_loop(1, 8, follow, 0)
-    pack([left[at] for at in range(55)], send_b, ROWS, lane)
+                ys[m, a] = y[a]
+                row = [left[m, 5 * a + b] for b in range(5)]
+                to_left[a] = to_left[a] + dot_vec(row, y)
+    pack(column + to_left, send_b, SOURCE, lane)
     start_b()
 
-    arrived_a()
     at_first = (sub_row == 0) & (lane < 32)
     at_last = (sub_row == 7) & (lane >= 96)
-    values = unpack(recv_a, ROWS, 55, lane)
-    for at in range(25):
-        sys[at] = jnp.where(at_first, 0.0, values[at])
-        sys[25 + at] = values[25 + at]
-    for a in range(5):
-        sys[75 + a] = values[50 + a]
-    arrived_b()
 
     def after(x, d):
         if d >= 8:
@@ -462,13 +478,22 @@
         x = pltpu.roll(x, d, 0)
         return jnp.where(sub_row < d, pltpu.roll(x, 32, 1), x)
 
-    values = unpack(recv_b, ROWS, 55, lane)
-    values = [jnp.where(at_last, 0.0, after(x, 1)) for x in values]
-    for at in range(25):
-        sys[50 + at] = values[at]
-        sys[25 + at] = sys[25 + at] + values[25 + at]
+    arrived_a()
+    values = unpack(recv_a, MATRIX, 105, lane)
+    last_cell = values[100:]
+    cell_before = [before(x, 1) for x in last_cell]
     for a in range(5):
-        sys[75 + a] = sys[75 + a] + values[50 + a]
+        low = times_jacobian(values[5 * a : 5 * a + 5], cell_before)
+        share = [jnp.where(at_last, 0.0, after(values[75 + 5 * a + b], 1)) for b in range(5)]
+        share = times_jacobian(share, last_cell)
+        for b in range(5):
+            sys[5 * a + b] = jnp.where(at_first, 0.0, low[b])
+            sys[25 + 5 * a + b] = values[25 + 5 * a + b] + share[b]
+            sys[50 + 5 * a + b] = jnp.where(at_last, 0.0, after(values[50 + 5 * a + b], 1))
+    arrived_b()
+    values = unpack(recv_b, SOURCE, 10, lane)
+    for a in range(5):
+        sys[75 + a] = values[a] + jnp.where(at_last, 0.0, after(values[5 + a], 1))
 
     for level in range(5):
         d = 1 << level
@@ -503,25 +528,24 @@
     factors = factor([[sys[25 + 5 * a + b] for b in range(5)] for a in range(5)])
     ends = solve(factors, [sys[75 + a] for a in range(5)])
     starts = [jnp.where(at_first, 0.0, before(x, 1)) for x in ends]
-    pack(ends + starts, send_c, BACK_ROWS, lane)
+    pack(ends + starts, send_c, BACK, lane)
     start_c()
     arrived_c()
-    values = unpack(recv_c, BACK_ROWS, 10, lane)
+    values = unpack(recv_c, BACK, 10, lane)
     for f in range(5):
         xs[CX, f] = values[f]
         xs[0, f] = values[5 + f]
 
-    def back(t, _):
-        m = 7 - t
-        x_left = [xs[0, f] for f in range(5)]
-        x_right = [xs[2 * m + 2, f] for f in range(5)]
+    g = apply_jacobian(cell(0), 1.0, [xs[0, f] for f in range(5)])
+    x_right = [xs[CX, f] for f in range(5)]
+    for m in reversed(range(7)):
+        x_here = []
         for a in range(5):
             row_f = [fac[m, 5 * a + b] for b in range(5)]
             row_s = [fac[m, 25 + 5 * a + b] for b in range(5)]
-            xs[2 * m, a] = fac[m, 50 + a] + (dot_vec(row_s, x_left) + dot_vec(row_f, x_right))
-        return 0
-
-    lax.fori_loop(0, 7, back, 0)
+            x_here.append((ys[m, a] + dot_vec(row_s, g)) + dot_vec(row_f, x_right))
+            xs[2 * m + 2, a] = x_here[a]
+        x_right = x_here
 
     def even(t, _):
         i = 2 * t + 1
@@ -540,6 +564,9 @@
             st[i, f] = new[f]
             lin[i, f] = flux[f]
         return 0
+
+    for copy in halos:
+        copy.wait_send()
 
     held = apply_jacobian(cell(CX - 1), 1.0, [xs[CX - 1, f] for f in range(5)])
     t = [rr[CX, f] + held[f] - (1.25 / 32.0) * xs[CX, f] for f in range(5)]
@@ -583,22 +610,22 @@
     return pl.pallas_call(
         kernel,
         out_shape=(jax.ShapeDtypeStruct(state.shape, F32), jax.ShapeDtypeStruct(state.shape, F32)),
-        in_specs=[pl.BlockSpec(memory_space=pltpu.VMEM)],
+        in_specs=[pl.BlockSpec(memory_space=pl.ANY)],
         out_specs=(pl.BlockSpec(memory_space=pltpu.VMEM), pl.BlockSpec(memory_space=pltpu.VMEM)),
         scratch_shapes=[
+            pltpu.VMEM(state.shape, F32),
             cells(CX + 2, 5), cells(CX + 2, 5), cells(CX + 2, 5), cells(CX + 2, 5),
-            cells(8, 55), cells(55), cells(5), cells(5), cells(5),
-            pltpu.VMEM((N * ROWS, 128), F32), pltpu.VMEM((N * ROWS, 128), F32),
-            pltpu.VMEM((N * ROWS, 128), F32), pltpu.VMEM((N * ROWS, 128), F32),
-            pltpu.VMEM((N * BACK_ROWS, 128), F32), pltpu.VMEM((N * BACK_ROWS, 128), F32),
+            cells(7, 50), cells(7, 5), cells(7, 30), cells(8, 25), cells(8, 50),
+            cells(5), cells(5), cells(5),
+            pltpu.VMEM((N * MATRIX[1], 128), F32), pltpu.VMEM((N * MATRIX[1], 128), F32),
+            pltpu.VMEM((N * SOURCE[1], 128), F32), pltpu.VMEM((N * SOURCE[1], 128), F32),
+            pltpu.VMEM((N * BACK[1], 128), F32), pltpu.VMEM((N * BACK[1], 128), F32),
             cells(80), cells(55), cells(CX + 2, 5), cells(CX + 2, 5),
-            pltpu.SemaphoreType.DMA((4,)), pltpu.SemaphoreType.DMA((4,)),
-            pltpu.SemaphoreType.DMA((N,)), pltpu.SemaphoreType.DMA((N,)),
-            pltpu.SemaphoreType.DMA((N,)), pltpu.SemaphoreType.DMA((N,)),
-            pltpu.SemaphoreType.DMA((N,)), pltpu.SemaphoreType.DMA((N,)),
+            pltpu.SemaphoreType.DMA, pltpu.SemaphoreType.DMA((4,)), pltpu.SemaphoreType.DMA((4,)),
+            pltpu.SemaphoreType.DMA((3,)), pltpu.SemaphoreType.DMA((3,)),
         ],
         compiler_params=pltpu.CompilerParams(
-            collective_id=0, has_side_effects=True, vmem_limit_bytes=32 * 1024 * 1024
+            collective_id=0, has_side_effects=True, vmem_limit_bytes=56 * 1024 * 1024
         ),
     )(state)
 

time: 47.2 us -> 38.3 us (0.81)
  Pallas kernels: 44 us -> 35 us
    pallas_call x1, Pallas kernels: 44 us -> 35 us  [on_device(): pl.pallas_call(kernel, out_shape=(jax.ShapeDtypeStruct(state.shape, F32),...]
where the time goes in v1:
time: 38.3 us; the launch traced here: 38.2 us
  Pallas kernels  35 us (91%)
  local copies, waits for them, and re-layouts  2.5 us (7%)
  between operations  0.65 us (2%)
    pallas_call x1, Pallas kernels, on_device(): pl.pallas_call(kernel, out_shape=(jax.ShapeDtypeStruct(state.shape, F32),...  35 us
    unnamed x4, local copies, waits for them, and re-layouts  2.5 us

profile of v1, /device:TPU:8, one launch (start us, length us, event | category | flops | bytes accessed | tf_op | source)
XLA Modules:
  0.0 38.2 jit_solution(16539259662512208427)
XLA Ops:
  0.6 35.0 %shard_map.30 = (f32[5,8,16,128]{3,2,1,0:T(8,128)}, f32[5,8,16,128]{3,2,1,0:T(8,128)}) custom-call(f32[5,8,16,128]{3,2,1,0:T(8,128)} %state_ref.1), custom_call_target="tpu_custom_call" | custom-call | tf_op jit(solution)/shard_map/pallas_call | solution.py:610
  35.7 0.0 copy-start
  35.7 1.8 %copy.5 = f32[5,8,16,128]{3,2,1,0:T(8,128)} copy(f32[5,8,16,128]{3,2,1,0:T(8,128)} %get-tuple-element.4) | data formatting | bytes 655360
  37.4 0.0 copy-done
  37.4 0.7 %copy.6 = f32[5,8,16,128]{3,2,1,0:T(8,128)} copy(f32[5,8,16,128]{3,2,1,0:T(8,128)S(1)} %copy-done) | data formatting | bytes 655360
Async XLA Ops:
  35.7 1.8 %copy-start = (f32[5,8,16,128]{3,2,1,0:T(8,128)S(1)}, f32[5,8,16,128]{3,2,1,0:T(8,128)}, u32[]{:S(2)}) copy-start(f32[5,8,16,128]{3,2,1,0:T(8,128)} %get-tuple-element.5) | copy-start | bytes 983044

commit v2 on v1

--- a/solution.py
+++ b/solution.py
@@ -12,10 +12,14 @@
 DISS = 1.0 / 256.0
 DIAG = 1.25 / 819.2
 PIVOTS = (1, 2, 3, 0, 4)
-MATRIX = (27, 32)
+OWN = (14, 16)
+SHARE = (13, 16)
 SOURCE = (3, 8)
 BACK = (3, 8)
 F32 = jnp.float32
+
+
+STEPS = [(dx, dz) for dz in (4, 3, 5, 2, 6, 1, 7, 0) for dx in (2, 1, 3, 0) if dx or dz]
 
 
 def mul(a, b):
@@ -214,30 +218,27 @@
 
 
 def kernel(
-    state_ref, next_ref, diff_ref,
-    here, st, pr, fx, rr, fac, ys, fct, lows, left, halo_send, halo_left, halo_right,
-    send_a, recv_a, send_b, recv_b, send_c, recv_c, sys, sol, xs, lin,
-    sem_in, ssem_h, rsem_h, ssem_x, rsem_x,
+    here, next_ref, diff_ref,
+    st, pr, fx, rr, fac, ys, fct, lows, left, halo_send, halo_left, halo_right,
+    send_a, recv_a, send_b, recv_b, send_r, recv_r, send_c, recv_c, sys, sol, fct2, xs, lin,
+    ssem_h, rsem_h, ssem_x, rsem_x,
 ):
     me = lax.axis_index("stream")
     mine = lax.axis_index("span")
-    span_right = lax.rem(mine + 1, SPAN)
-    span_left = lax.rem(mine + SPAN - 1, SPAN)
+    span_right = (mine + 1) & (SPAN - 1)
+    span_left = (mine + SPAN - 1) & (SPAN - 1)
 
     barrier = pltpu.get_barrier_semaphore()
-    load = pltpu.make_async_copy(state_ref, here, sem_in)
-    load.start()
+
+    def stepped(dx, dz):
+        return (((me >> 3) + dx) & 3) * 8 + ((me + dz) & 7)
+
+    for step in STEPS:
+        pl.semaphore_signal(
+            barrier, inc=1, device_id=(stepped(*step), mine), device_id_type=MESH
+        )
     for other in (span_left, span_right):
         pl.semaphore_signal(barrier, inc=1, device_id={"span": other}, device_id_type=MESH)
-
-    def greet(d, _):
-        pl.semaphore_signal(
-            barrier, inc=1, device_id={"stream": lax.rem(me + d, N)}, device_id_type=MESH
-        )
-        return 0
-
-    lax.fori_loop(1, N, greet, 0)
-    load.wait()
 
     lane = lax.broadcasted_iota(jnp.int32, (8, 128), 1)
     sub_row = lax.broadcasted_iota(jnp.int32, (8, 128), 0)
@@ -312,28 +313,7 @@
             lows[7, 5 * a + b] = low[a][b]
             value = full(own[a][b]) - dot_row(low[a], f_last, b)
             to_own.append(value + DIAG if a == b else value)
-    pack((to_low + to_own)[:48], send_a, MATRIX, lane)
-
-    upper = product(cell(1), -1.0, cell(2), -1.0)
-    columns = jacobian_columns(cell(1), -1.0)
-    for a in range(5):
-        for b in range(5):
-            left[0, 5 * a + b] = full(upper[a][b])
-            left[0, 25 + 5 * a + b] = full(columns[b][a])
-
-    def follow(m, _):
-        f_here = [[fac[m, 5 * a + b] for b in range(5)] for a in range(5)]
-        s_here = [[fac[m, 25 + 5 * a + b] for b in range(5)] for a in range(5)]
-        for a in range(5):
-            row = [left[m, 5 * a + b] for b in range(5)]
-            for b in range(5):
-                left[m + 1, 25 + 5 * a + b] = left[m, 25 + 5 * a + b] - dot_row(row, s_here, b)
-                left[m + 1, 5 * a + b] = dot_row(row, f_here, b)
-        return 0
-
-    lax.fori_loop(0, 7, follow, 0)
-    rest = to_own[-2:] + [left[7, at] for at in range(50)] + list(cell(CX))
-    pack(rest, send_a, MATRIX, lane, 12)
+    pack(to_low + to_own + list(cell(CX)), send_a, OWN, lane)
 
     for f in range(5):
         packed = st[1, f]
@@ -347,8 +327,8 @@
     halos = []
     for at, (src, dst, who) in enumerate(
         (
-            (st.at[CX], st.at[0], {"stream": lax.rem(me + 1, N)}),
-            (st.at[1], st.at[CX + 1], {"stream": lax.rem(me + N - 1, N)}),
+            (st.at[CX], st.at[0], {"stream": (me + 1) & (N - 1)}),
+            (st.at[1], st.at[CX + 1], {"stream": (me + N - 1) & (N - 1)}),
             (halo_send, halo_left, {"span": span_right}),
             (halo_send, halo_right, {"span": span_left}),
         )
@@ -364,17 +344,16 @@
         count, stride = rows
 
         def start():
-            def body(d, _):
-                other = lax.rem(me + d, N)
+            def send_to(other):
                 pltpu.make_async_remote_copy(
                     src_ref=send.at[pl.ds(pl.multiple_of(other * stride, 8), count)],
                     dst_ref=recv.at[pl.ds(pl.multiple_of(me * stride, 8), count)],
                     send_sem=ssem_x.at[at], recv_sem=rsem_x.at[at],
-                    device_id={"stream": other}, device_id_type=MESH,
+                    device_id=(other, mine), device_id_type=MESH,
                 ).start()
-                return 0
-
-            lax.fori_loop(1, N, body, 0)
+
+            for step in STEPS:
+                send_to(stepped(*step))
             place = pl.ds(pl.multiple_of(me * stride, 8), stride)
             recv[place, :] = send[place, :]
 
@@ -382,14 +361,36 @@
             src_ref=send.at[pl.ds(0, (N - 1) * count)],
             dst_ref=recv.at[pl.ds(0, (N - 1) * count)],
             send_sem=ssem_x.at[at], recv_sem=rsem_x.at[at],
-            device_id={"stream": lax.rem(me + 1, N)}, device_id_type=MESH,
+            device_id=((me + 1) & (N - 1), mine), device_id_type=MESH,
         )
         return start, everything.wait_recv, everything.wait_send
 
-    start_a, arrived_a, sent_a = exchange(send_a, recv_a, 0, MATRIX)
-    start_b, arrived_b, sent_b = exchange(send_b, recv_b, 1, SOURCE)
-    start_c, arrived_c, sent_c = exchange(send_c, recv_c, 2, BACK)
+    start_a, arrived_a, sent_a = exchange(send_a, recv_a, 0, OWN)
+    start_b, arrived_b, sent_b = exchange(send_b, recv_b, 1, SHARE)
+    start_r, arrived_r, sent_r = exchange(send_r, recv_r, 2, SOURCE)
+    start_c, arrived_c, sent_c = exchange(send_c, recv_c, 3, BACK)
     start_a()
+
+    upper = product(cell(1), -1.0, cell(2), -1.0)
+    columns = jacobian_columns(cell(1), -1.0)
+    for a in range(5):
+        for b in range(5):
+            left[0, 5 * a + b] = full(upper[a][b])
+            left[0, 25 + 5 * a + b] = full(columns[b][a])
+
+    def follow(m, _):
+        f_here = [[fac[m, 5 * a + b] for b in range(5)] for a in range(5)]
+        s_here = [[fac[m, 25 + 5 * a + b] for b in range(5)] for a in range(5)]
+        for a in range(5):
+            row = [left[m, 5 * a + b] for b in range(5)]
+            for b in range(5):
+                left[m + 1, 25 + 5 * a + b] = left[m, 25 + 5 * a + b] - dot_row(row, s_here, b)
+                left[m + 1, 5 * a + b] = dot_row(row, f_here, b)
+        return 0
+
+    lax.fori_loop(0, 7, follow, 0)
+    pack([left[7, at] for at in range(50)], send_b, SHARE, lane)
+    start_b()
 
     for copy in halos:
         copy.wait_recv()
@@ -460,8 +461,8 @@
                 ys[m, a] = y[a]
                 row = [left[m, 5 * a + b] for b in range(5)]
                 to_left[a] = to_left[a] + dot_vec(row, y)
-    pack(column + to_left, send_b, SOURCE, lane)
-    start_b()
+    pack(column + to_left, send_r, SOURCE, lane)
+    start_r()
 
     at_first = (sub_row == 0) & (lane < 32)
     at_last = (sub_row == 7) & (lane >= 96)
@@ -479,54 +480,63 @@
         return jnp.where(sub_row < d, pltpu.roll(x, 32, 1), x)
 
     arrived_a()
-    values = unpack(recv_a, MATRIX, 105, lane)
-    last_cell = values[100:]
+    values = unpack(recv_a, OWN, 55, lane)
+    last_cell = values[50:]
     cell_before = [before(x, 1) for x in last_cell]
     for a in range(5):
         low = times_jacobian(values[5 * a : 5 * a + 5], cell_before)
-        share = [jnp.where(at_last, 0.0, after(values[75 + 5 * a + b], 1)) for b in range(5)]
+        for b in range(5):
+            sys[5 * a + b] = jnp.where(at_first, 0.0, low[b])
+            sys[25 + 5 * a + b] = values[25 + 5 * a + b]
+    arrived_b()
+    values = unpack(recv_b, SHARE, 50, lane)
+    for a in range(5):
+        share = [jnp.where(at_last, 0.0, after(values[25 + 5 * a + b], 1)) for b in range(5)]
         share = times_jacobian(share, last_cell)
         for b in range(5):
-            sys[5 * a + b] = jnp.where(at_first, 0.0, low[b])
-            sys[25 + 5 * a + b] = values[25 + 5 * a + b] + share[b]
-            sys[50 + 5 * a + b] = jnp.where(at_last, 0.0, after(values[50 + 5 * a + b], 1))
-    arrived_b()
-    values = unpack(recv_b, SOURCE, 10, lane)
-    for a in range(5):
-        sys[75 + a] = values[a] + jnp.where(at_last, 0.0, after(values[5 + a], 1))
+            sys[25 + 5 * a + b] = sys[25 + 5 * a + b] + share[b]
+            sys[50 + 5 * a + b] = jnp.where(at_last, 0.0, after(values[5 * a + b], 1))
 
     for level in range(5):
         d = 1 << level
         factors = factor([[sys[25 + 5 * a + b] for b in range(5)] for a in range(5)])
+        keep_factors(factors, fct2, level)
         for b in range(5):
             x = solve(factors, [sys[5 * a + b] for a in range(5)])
             for a in range(5):
-                sol[5 * a + b] = x[a]
+                sol[level, 5 * a + b] = x[a]
             x = solve(factors, [sys[50 + 5 * a + b] for a in range(5)])
             for a in range(5):
-                sol[25 + 5 * a + b] = x[a]
-        x = solve(factors, [sys[75 + a] for a in range(5)])
-        for a in range(5):
-            sol[50 + a] = x[a]
-        lows = [[sol[5 * a + b] for b in range(5)] for a in range(5)]
-        ups = [[sol[25 + 5 * a + b] for b in range(5)] for a in range(5)]
-        for b in range(5):
-            low_column = [[before(sol[5 * a + b], d)] for a in range(5)]
-            up_column = [[after(sol[25 + 5 * a + b], d)] for a in range(5)]
-            cross_low = [[before(sol[25 + 5 * a + b], d)] for a in range(5)]
-            cross_up = [[after(sol[5 * a + b], d)] for a in range(5)]
+                sol[level, 25 + 5 * a + b] = x[a]
+        low = [[sol[level, 5 * a + b] for b in range(5)] for a in range(5)]
+        up = [[sol[level, 25 + 5 * a + b] for b in range(5)] for a in range(5)]
+        for b in range(5):
+            low_column = [[before(low[a][b], d)] for a in range(5)]
+            up_column = [[after(up[a][b], d)] for a in range(5)]
+            cross_low = [[before(up[a][b], d)] for a in range(5)]
+            cross_up = [[after(low[a][b], d)] for a in range(5)]
             for a in range(5):
-                value = -(dot_row(lows[a], cross_low, 0) + dot_row(ups[a], cross_up, 0))
+                value = -(dot_row(low[a], cross_low, 0) + dot_row(up[a], cross_up, 0))
                 sys[25 + 5 * a + b] = value + 1.0 if a == b else value
                 if level < 4:
-                    sys[5 * a + b] = dot_row(lows[a], low_column, 0)
-                    sys[50 + 5 * a + b] = dot_row(ups[a], up_column, 0)
-        r_low = [before(sol[50 + a], d) for a in range(5)]
-        r_high = [after(sol[50 + a], d) for a in range(5)]
+                    sys[5 * a + b] = dot_row(low[a], low_column, 0)
+                    sys[50 + 5 * a + b] = dot_row(up[a], up_column, 0)
+    factors = factor([[sys[25 + 5 * a + b] for b in range(5)] for a in range(5)])
+
+    arrived_r()
+    values = unpack(recv_r, SOURCE, 10, lane)
+    r = [values[a] + jnp.where(at_last, 0.0, after(values[5 + a], 1)) for a in range(5)]
+    for level in range(5):
+        d = 1 << level
+        x = solve(kept_factors(fct2, level), r)
+        x_low = [before(x[a], d) for a in range(5)]
+        x_high = [after(x[a], d) for a in range(5)]
+        r = []
         for a in range(5):
-            sys[75 + a] = sol[50 + a] + dot_vec(lows[a], r_low) + dot_vec(ups[a], r_high)
-    factors = factor([[sys[25 + 5 * a + b] for b in range(5)] for a in range(5)])
-    ends = solve(factors, [sys[75 + a] for a in range(5)])
+            low = [sol[level, 5 * a + b] for b in range(5)]
+            up = [sol[level, 25 + 5 * a + b] for b in range(5)]
+            r.append(x[a] + (dot_vec(low, x_low) + dot_vec(up, x_high)))
+    ends = solve(factors, r)
     starts = [jnp.where(at_first, 0.0, before(x, 1)) for x in ends]
     pack(ends + starts, send_c, BACK, lane)
     start_c()
@@ -600,6 +610,7 @@
 
     sent_a()
     sent_b()
+    sent_r()
     sent_c()
 
 
@@ -610,22 +621,22 @@
     return pl.pallas_call(
         kernel,
         out_shape=(jax.ShapeDtypeStruct(state.shape, F32), jax.ShapeDtypeStruct(state.shape, F32)),
-        in_specs=[pl.BlockSpec(memory_space=pl.ANY)],
+        in_specs=[pl.BlockSpec(memory_space=pltpu.VMEM)],
         out_specs=(pl.BlockSpec(memory_space=pltpu.VMEM), pl.BlockSpec(memory_space=pltpu.VMEM)),
         scratch_shapes=[
-            pltpu.VMEM(state.shape, F32),
             cells(CX + 2, 5), cells(CX + 2, 5), cells(CX + 2, 5), cells(CX + 2, 5),
             cells(7, 50), cells(7, 5), cells(7, 30), cells(8, 25), cells(8, 50),
             cells(5), cells(5), cells(5),
-            pltpu.VMEM((N * MATRIX[1], 128), F32), pltpu.VMEM((N * MATRIX[1], 128), F32),
+            pltpu.VMEM((N * OWN[1], 128), F32), pltpu.VMEM((N * OWN[1], 128), F32),
+            pltpu.VMEM((N * SHARE[1], 128), F32), pltpu.VMEM((N * SHARE[1], 128), F32),
             pltpu.VMEM((N * SOURCE[1], 128), F32), pltpu.VMEM((N * SOURCE[1], 128), F32),
             pltpu.VMEM((N * BACK[1], 128), F32), pltpu.VMEM((N * BACK[1], 128), F32),
-            cells(80), cells(55), cells(CX + 2, 5), cells(CX + 2, 5),
-            pltpu.SemaphoreType.DMA, pltpu.SemaphoreType.DMA((4,)), pltpu.SemaphoreType.DMA((4,)),
-            pltpu.SemaphoreType.DMA((3,)), pltpu.SemaphoreType.DMA((3,)),
+            cells(75), cells(5, 50), cells(5, 30), cells(CX + 2, 5), cells(CX + 2, 5),
+            pltpu.SemaphoreType.DMA((4,)), pltpu.SemaphoreType.DMA((4,)),
+            pltpu.SemaphoreType.DMA((4,)), pltpu.SemaphoreType.DMA((4,)),
         ],
         compiler_params=pltpu.CompilerParams(
-            collective_id=0, has_side_effects=True, vmem_limit_bytes=56 * 1024 * 1024
+            collective_id=0, has_side_effects=True, vmem_limit_bytes=24 * 1024 * 1024
         ),
     )(state)
 

time: 38.3 us -> 35.6 us (0.930)
  Pallas kernels: 35 us -> 32.4 us
    pallas_call x1, Pallas kernels: 35 us -> 32.4 us  [on_device(): pl.pallas_call(kernel, out_shape=(jax.ShapeDtypeStruct(state.shape, F32),...]
where the time goes in v2:
time: 35.6 us; the launch traced here: 35.4 us
  Pallas kernels  32.4 us (91%)
  local copies, waits for them, and re-layouts  2.42 us (7%)
  between operations  0.65 us (2%)
    pallas_call x1, Pallas kernels, on_device(): pl.pallas_call(kernel, out_shape=(jax.ShapeDtypeStruct(state.shape, F32),...  32.4 us
    unnamed x4, local copies, waits for them, and re-layouts  2.42 us

profile of v2, /device:TPU:8, one launch (start us, length us, event | category | flops | bytes accessed | tf_op | source)
XLA Modules:
  0.0 35.4 jit_solution(7998813556676794253)
XLA Ops:
  0.6 0.0 copy-start
  0.6 1.0 %copy-done = f32[5,8,16,128]{3,2,1,0:T(8,128)S(1)} copy-done((f32[5,8,16,128]{3,2,1,0:T(8,128)S(1)}, f32[5,8,16,128]{3,2,1,0:T(8,128)}, u32[]{:S(2)}) %copy-start) | copy-done | bytes 327704
  1.6 32.4 %shard_map.30 = (f32[5,8,16,128]{3,2,1,0:T(8,128)S(1)}, f32[5,8,16,128]{3,2,1,0:T(8,128)S(1)}) custom-call(f32[5,8,16,128]{3,2,1,0:T(8,128)S(1)} %copy-done), custom_call_target="tpu_custom_call" | custom-call | tf_op jit(solution)/shard_map/pallas_call | solution.py:621
  34.0 0.7 %copy.5 = f32[5,8,16,128]{3,2,1,0:T(8,128)} copy(f32[5,8,16,128]{3,2,1,0:T(8,128)S(1)} %get-tuple-element.4) | data formatting | bytes 655360
  34.7 0.7 %copy.6 = f32[5,8,16,128]{3,2,1,0:T(8,128)} copy(f32[5,8,16,128]{3,2,1,0:T(8,128)S(1)} %get-tuple-element.5) | data formatting | bytes 655360
Async XLA Ops:
  0.6 1.0 %copy-start = (f32[5,8,16,128]{3,2,1,0:T(8,128)S(1)}, f32[5,8,16,128]{3,2,1,0:T(8,128)}, u32[]{:S(2)}) copy-start(f32[5,8,16,128]{3,2,1,0:T(8,128)} %here.1) | copy-start | bytes 983044

commit v3 on v2

--- a/solution.py
+++ b/solution.py
@@ -197,7 +197,7 @@
     return [c0, c1, c2, c3]
 
 
-def pack(values, ref, rows, lane, first=0):
+def pack(values, ref, rows, lane, places=(8, 1)):
     values = list(values)
     rows = rows[1]
     while len(values) % 4:
@@ -205,20 +205,22 @@
     for g in range(len(values) // 4):
         out = quarters(values[4 * g : 4 * g + 4], lane)
         for t in range(4):
-            ref[pl.ds(8 * t * rows + first + g, 8, stride=rows), :] = out[t]
-
-
-def unpack(ref, rows, count, lane):
+            ref[pl.ds(places[0] * t * rows + g, 8, stride=places[1] * rows), :] = out[t]
+
+
+def unpack(ref, rows, count, lane, places=(8, 1)):
     values = []
     rows = rows[1]
     for g in range((count + 3) // 4):
-        got = [ref[pl.ds(8 * t * rows + g, 8, stride=rows), :] for t in range(4)]
+        got = [
+            ref[pl.ds(places[0] * t * rows + g, 8, stride=places[1] * rows), :] for t in range(4)
+        ]
         values += quarters(got, lane)
     return values[:count]
 
 
 def kernel(
-    here, next_ref, diff_ref,
+    here, out_ref,
     st, pr, fx, rr, fac, ys, fct, lows, left, halo_send, halo_left, halo_right,
     send_a, recv_a, send_b, recv_b, send_r, recv_r, send_c, recv_c, sys, sol, fct2, xs, lin,
     ssem_h, rsem_h, ssem_x, rsem_x,
@@ -468,19 +470,19 @@
     at_last = (sub_row == 7) & (lane >= 96)
 
     def after(x, d):
-        if d >= 8:
-            return pltpu.roll(x, 128 - 4 * d, 1)
-        x = pltpu.roll(x, 8 - d, 0)
-        return jnp.where(sub_row >= 8 - d, pltpu.roll(x, 96, 1), x)
+        if d >= 4:
+            return pltpu.roll(x, 8 - d // 4, 0)
+        x = pltpu.roll(x, 128 - 32 * d, 1)
+        return jnp.where(lane >= 128 - 32 * d, pltpu.roll(x, 7, 0), x)
 
     def before(x, d):
-        if d >= 8:
-            return pltpu.roll(x, 4 * d, 1)
-        x = pltpu.roll(x, d, 0)
-        return jnp.where(sub_row < d, pltpu.roll(x, 32, 1), x)
+        if d >= 4:
+            return pltpu.roll(x, d // 4, 0)
+        x = pltpu.roll(x, 32 * d, 1)
+        return jnp.where(lane < 32 * d, pltpu.roll(x, 1, 0), x)
 
     arrived_a()
-    values = unpack(recv_a, OWN, 55, lane)
+    values = unpack(recv_a, OWN, 55, lane, (1, 4))
     last_cell = values[50:]
     cell_before = [before(x, 1) for x in last_cell]
     for a in range(5):
@@ -489,7 +491,7 @@
             sys[5 * a + b] = jnp.where(at_first, 0.0, low[b])
             sys[25 + 5 * a + b] = values[25 + 5 * a + b]
     arrived_b()
-    values = unpack(recv_b, SHARE, 50, lane)
+    values = unpack(recv_b, SHARE, 50, lane, (1, 4))
     for a in range(5):
         share = [jnp.where(at_last, 0.0, after(values[25 + 5 * a + b], 1)) for b in range(5)]
         share = times_jacobian(share, last_cell)
@@ -524,7 +526,7 @@
     factors = factor([[sys[25 + 5 * a + b] for b in range(5)] for a in range(5)])
 
     arrived_r()
-    values = unpack(recv_r, SOURCE, 10, lane)
+    values = unpack(recv_r, SOURCE, 10, lane, (1, 4))
     r = [values[a] + jnp.where(at_last, 0.0, after(values[5 + a], 1)) for a in range(5)]
     for level in range(5):
         d = 1 << level
@@ -538,7 +540,7 @@
             r.append(x[a] + (dot_vec(low, x_low) + dot_vec(up, x_high)))
     ends = solve(factors, r)
     starts = [jnp.where(at_first, 0.0, before(x, 1)) for x in ends]
-    pack(ends + starts, send_c, BACK, lane)
+    pack(ends + starts, send_c, BACK, lane, (1, 4))
     start_c()
     arrived_c()
     values = unpack(recv_c, BACK, 10, lane)
@@ -605,8 +607,8 @@
     for f in range(5):
         for half in range(2):
             place = pl.ds(8 * half, 8)
-            next_ref[f, :, place, :] = jnp.swapaxes(st[pl.ds(1 + 8 * half, 8), f], 0, 1)
-            diff_ref[f, :, place, :] = jnp.swapaxes(xs[pl.ds(1 + 8 * half, 8), f], 0, 1)
+            out_ref[0, f, :, place, :] = jnp.swapaxes(st[pl.ds(1 + 8 * half, 8), f], 0, 1)
+            out_ref[1, f, :, place, :] = jnp.swapaxes(xs[pl.ds(1 + 8 * half, 8), f], 0, 1)
 
     sent_a()
     sent_b()
@@ -618,11 +620,11 @@
     def cells(*shape):
         return pltpu.VMEM(shape + (8, 128), F32)
 
-    return pl.pallas_call(
+    both = pl.pallas_call(
         kernel,
-        out_shape=(jax.ShapeDtypeStruct(state.shape, F32), jax.ShapeDtypeStruct(state.shape, F32)),
+        out_shape=jax.ShapeDtypeStruct((2,) + state.shape, F32),
         in_specs=[pl.BlockSpec(memory_space=pltpu.VMEM)],
-        out_specs=(pl.BlockSpec(memory_space=pltpu.VMEM), pl.BlockSpec(memory_space=pltpu.VMEM)),
+        out_specs=pl.BlockSpec(memory_space=pltpu.VMEM),
         scratch_shapes=[
             cells(CX + 2, 5), cells(CX + 2, 5), cells(CX + 2, 5), cells(CX + 2, 5),
             cells(7, 50), cells(7, 5), cells(7, 30), cells(8, 25), cells(8, 50),
@@ -639,6 +641,7 @@
             collective_id=0, has_side_effects=True, vmem_limit_bytes=24 * 1024 * 1024
         ),
     )(state)
+    return both[0], both[1]
 
 
 def solution(mesh):

time: 35.6 us -> 34.8 us (0.978)
  local copies, waits for them, and re-layouts: 2.42 us -> 1.84 us
    unnamed x4 -> x2, local copies, waits for them, and re-layouts: 2.42 us -> 0.97 us
    squeeze x0 -> x1, local copies, waits for them, and re-layouts: none -> 0.88 us  [on_device(): return (both[0], both[1])]
where the time goes in v3:
time: 34.8 us; the launch traced here: 34.7 us
  Pallas kernels  32.2 us (93%)
  local copies, waits for them, and re-layouts  1.84 us (5%)
  between operations  0.65 us (2%)
    pallas_call x1, Pallas kernels, on_device(): pl.pallas_call(kernel, out_shape=jax.ShapeDtypeStruct((2,) + state.shape,...  32.2 us
    unnamed x2, local copies, waits for them, and re-layouts  0.97 us
    squeeze x1, local copies, waits for them, and re-layouts, on_device(): return (both[0], both[1])  0.88 us

profile of v3, /device:TPU:8, one launch (start us, length us, event | category | flops | bytes accessed | tf_op | source)
XLA Modules:
  0.0 34.7 jit_solution(10290611684775955833)
XLA Ops:
  0.6 0.0 copy-start
  0.6 1.0 %copy-done = f32[5,8,16,128]{3,2,1,0:T(8,128)S(1)} copy-done((f32[5,8,16,128]{3,2,1,0:T(8,128)S(1)}, f32[5,8,16,128]{3,2,1,0:T(8,128)}, u32[]{:S(2)}) %copy-start) | copy-done | bytes 327704
  1.6 32.2 %shard_map.30 = f32[2,5,8,16,128]{4,3,2,1,0:T(8,128)S(1)} custom-call(f32[5,8,16,128]{3,2,1,0:T(8,128)S(1)} %copy-done), custom_call_target="tpu_custom_call" | custom-call | tf_op jit(solution)/shard_map/pallas_call | solution.py:623
  33.8 0.9 %slice_bitcast_fusion = (f32[5,8,16,128]{3,2,1,0:T(8,128)}, f32[5,8,16,128]{3,2,1,0:T(8,128)}) fusion(f32[2,5,8,16,128]{4,3,2,1,0:T(8,128)S(1)} %shard_map.30), kind=kLoop, calls=%fused_computation | loop fusion | bytes 1310720 | tf_op jit(solution)/shard_map/squeeze | solution.py:644
Async XLA Ops:
  0.6 1.0 %copy-start = (f32[5,8,16,128]{3,2,1,0:T(8,128)S(1)}, f32[5,8,16,128]{3,2,1,0:T(8,128)}, u32[]{:S(2)}) copy-start(f32[5,8,16,128]{3,2,1,0:T(8,128)} %here.1) | copy-start | bytes 983044
